TPU v7x, 32 devices: a whole 2x2x4 slice. The times are simulated.
32 devices in a mesh: groups: 2 (over y), blk: 16 (over z, x, core).
Axes of the slice: x: 2, y: 2, z: 4, core: 2. Of those that a mesh axis runs over, the one named last changes fastest.
Arguments:
- snapshots: bfloat16 [64, 64, 16, 128], P(None, ('groups', 'blk')), parts along dimension 1, may hold values from -200 to 200
- old_modes: bfloat16 [192, 64, 16, 128], P(None, ('groups', 'blk')), parts along dimension 1, may hold values from -60 to 60
- mode_scales: float32 [384], P('groups'), parts along dimension 0, may hold values from 0.3 to 3
- plane_counts: int32 [32], P(('groups', 'blk')), parts along dimension 0, may hold values from 1 to 2, 20 in all
- links: int32 [32, 2], P(('groups', 'blk')), parts along dimension 0, may hold values from 0 to 1, as said below
Outputs:
- new_modes: bfloat16 [256, 64, 16, 128], P(None, ('groups', 'blk')), parts along dimension 1
- factor: float32 [512, 256], P('groups'), parts along dimension 0
There are 2 independent parts, one for each index of `groups`. A program takes and returns all parts, laid end to end along the dimension named above; each array names one. Nothing has to cross between parts.
Inputs may be any that keep to these rules, and one draw needn't show every extreme that they name: links[b, 1] equals links[b + 1 mod 16, 0]; 1 joins two blocks, 0 is a wall.
All inputs are finite; a program needn't handle non-finite values. No bound on the sum of `plane_counts` on one device may be relied on, other than what follows from the above.
Results may differ from a plain program's by a relative error of at most 0.0095.
Values may be sent and summed in bfloat16 or wider, within the bound.
A program may use at most 128 MiB of HBM per device.

v0:
```python
import jax
import jax.numpy as jnp
from jax import lax
from jax.sharding import PartitionSpec as P


def with_halo(x, sides, width):
    for axis, dim in sides:
        peers, length = (lax.axis_size(axis), x.shape[dim])
        up = [(i, (i + 1) % peers) for i in range(peers)]
        down = [(j, i) for i, j in up]
        last = lax.slice_in_dim(x, length - width, length, axis=dim)
        leading = lax.slice_in_dim(x, 0, width, axis=dim)
        before = lax.ppermute(last, axis, up)
        after = lax.ppermute(leading, axis, down)
        x = jnp.concatenate([before, x, after], axis=dim)
    return x


def smooth_along(field, along):
    widths = [(0, 0)] * field.ndim
    widths[along] = (1, 1)
    padded = jnp.pad(field, widths)
    length = field.shape[along]
    lower = lax.slice_in_dim(padded, 0, length, axis=along)
    upper = lax.slice_in_dim(padded, 2, length + 2, axis=along)
    return 0.25 * lower + 0.5 * field + 0.25 * upper


def gram_term(left_rows, right_rows):
    return lax.dot_general(
        left_rows, right_rows, (((1,), (1,)), ((), ())), preferred_element_type=jnp.float32
    )


def exact_dot(left_mat, right_mat):
    return jnp.dot(left_mat, right_mat, precision=lax.Precision.HIGHEST)


def leaf_factor(matrix):
    order = matrix.shape[0]
    row_ids = lax.iota(jnp.int32, order)
    lower = jnp.zeros((order, order), jnp.float32)
    for column in range(order):
        residue = matrix[:, column] - exact_dot(lower, lower[column, :])
        pivot = jnp.sqrt(residue[column])
        lower = lower.at[:, column].set(jnp.where(row_ids >= column, residue / pivot, 0.0))
    inverse = jnp.zeros((order, order), jnp.float32)
    for row in range(order):
        target = jnp.zeros((order,), jnp.float32).at[row].set(1.0)
        solved = (target - exact_dot(lower[row, :], inverse)) / lower[row, row]
        inverse = inverse.at[row, :].set(solved)
    return (lower, inverse)


def lower_factor(matrix):
    order = matrix.shape[0]
    if order <= 8:
        return leaf_factor(matrix)
    half = order // 2
    lower_one, inverse_one = lower_factor(matrix[:half, :half])
    below = exact_dot(matrix[half:, :half], inverse_one.T)
    rest = matrix[half:, half:] - exact_dot(below, below.T)
    lower_two, inverse_two = lower_factor(rest)
    corner = -exact_dot(inverse_two, exact_dot(below, inverse_one))
    top_zero = jnp.zeros((half, order - half), jnp.float32)
    lower = jnp.concatenate(
        [
            jnp.concatenate([lower_one, top_zero], axis=1),
            jnp.concatenate([below, lower_two], axis=1),
        ],
        axis=0,
    )
    inverse = jnp.concatenate(
        [
            jnp.concatenate([inverse_one, top_zero], axis=1),
            jnp.concatenate([corner, inverse_two], axis=1),
        ],
        axis=0,
    )
    return (lower, inverse)


def shards(snapshots, old_modes, mode_scales, plane_counts, links):
    new_count, plane_slots, rows_y, rows_z = snapshots.shape
    keep_count = old_modes.shape[0]
    columns = new_count + keep_count
    plane_count = plane_counts[0]
    plane_ids = lax.iota(jnp.int32, plane_slots)
    alive_mask = (plane_ids < plane_count).astype(jnp.float32)[None, :, None, None]
    last_pick = (plane_ids == plane_count - 1).astype(jnp.float32)[None, :, None, None]
    masked = snapshots.astype(jnp.float32) * alive_mask
    first_plane = masked[:, 0]
    last_plane = jnp.sum(masked * last_pick, axis=1)
    edge_planes = jnp.stack([first_plane, last_plane], axis=1).astype(jnp.bfloat16)
    widened = with_halo(edge_planes, (("blk", 1),), 1)
    left_halo = widened[:, 0].astype(jnp.float32) * links[0, 0].astype(jnp.float32)
    right_halo = widened[:, 3].astype(jnp.float32) * links[0, 1].astype(jnp.float32)
    behind = jnp.concatenate([left_halo[:, None], masked[:, :-1]], axis=1)
    forward = jnp.concatenate([masked[:, 1:], jnp.zeros_like(masked[:, :1])], axis=1)
    forward = forward + last_pick * right_halo[:, None]
    along_planes = 0.25 * behind + 0.5 * masked + 0.25 * forward
    filtered = (smooth_along(smooth_along(along_planes, 2), 3) * alive_mask).astype(jnp.bfloat16)
    scaled = (mode_scales[:, None, None, None] * old_modes.astype(jnp.float32) * alive_mask).astype(
        jnp.bfloat16
    )
    stacked = jnp.concatenate([filtered, scaled], axis=0).reshape(
        columns, plane_slots * rows_y * rows_z
    )
    cell_total = lax.axis_size("blk") * stacked.shape[1]
    local_gram = gram_term(stacked, stacked)
    gram = lax.psum(local_gram, "blk") / cell_total
    lower, inverse_lower = lower_factor(gram)
    factor = lower.T
    inverse_high = inverse_lower.astype(jnp.bfloat16)
    inverse_low = (inverse_lower - inverse_high.astype(jnp.float32)).astype(jnp.bfloat16)
    result = jnp.dot(inverse_high, stacked, preferred_element_type=jnp.float32)
    result = result + jnp.dot(inverse_low, stacked, preferred_element_type=jnp.float32)
    return (result.reshape(columns, plane_slots, rows_y, rows_z).astype(jnp.bfloat16), factor)


def solution(mesh):
    return jax.shard_map(
        shards,
        mesh=mesh,
        in_specs=(
            P(None, ("groups", "blk"), None, None),
            P(None, ("groups", "blk"), None, None),
            P("groups"),
            P(("groups", "blk")),
            P(("groups", "blk"), None),
        ),
        out_specs=(P(None, ("groups", "blk"), None, None), P("groups", None)),
        check_vma=False,
    )
```

profile of v0, /device:TPU:1, one launch (start us, length us, event | category | flops | bytes accessed | tf_op | source)
XLA Modules:
  0.0 922.3 jit_solution(12888956410553050702)
XLA Ops:
  7.9 1.4 multiply_reduce_fusion
  9.5 2.6 collective-permute-start
  21.0 1.4 convolution_bitcast_fusion
  22.4 1.5 pad_maximum_fusion
  24.0 2.9 copy.589
  26.9 88.5 %all-reduce.131.cloned.1.call-done = f32[256,256]{1,0:T(8,128)} async-done(((f32[256,256]{1,0:T(8,128)}), f32[256,256]{1,0:T(8,128)}) %all-reduce.131.cloned.1.call-update) | async-done | bytes 262160 | tf_op jit(solution)/shard_map/psum | solution.py:112
  115.4 1.0 broadcast_multiply_fusion
  139.8 0.8 fusion.32
  161.9 0.8 fusion.54
  162.8 0.8 fusion.57
  188.9 0.8 fusion.94
  213.8 0.8 fusion.125
  238.6 0.8 fusion.156
  260.8 0.8 fusion.178
  287.0 0.8 fusion.215
  287.8 0.8 fusion.218
  311.8 0.8 fusion.246
  312.6 0.8 fusion.249
  336.5 0.8 fusion.274
  338.1 0.8 fusion.280
  360.3 0.8 fusion.302
  361.1 0.8 fusion.305
  385.7 0.8 fusion.336
  387.3 0.8 fusion.342
  411.2 0.8 fusion.370
  412.0 0.8 fusion.373
  436.8 0.8 fusion.404
  459.1 0.8 fusion.426
  486.1 0.8 fusion.466
  511.1 0.8 fusion.497
  536.7 0.8 fusion.528
  558.8 0.8 fusion.550
  586.1 0.8 fusion.590
  610.7 0.8 fusion.621
  635.6 0.8 fusion.652
  657.7 0.8 fusion.674
  684.7 0.8 fusion.714
  710.0 0.8 fusion.745
  735.1 0.8 fusion.776
  757.3 0.8 fusion.798
  784.3 0.8 fusion.838
  808.9 0.8 fusion.869
  834.1 0.8 fusion.900
  856.2 0.8 fusion.922
  883.4 0.8 fusion.962
  908.8 0.8 fusion.993
  910.0 0.8 copy.591
  913.4 1.8 copy.625
  (2228 shorter events, 610.3 us)
Async XLA Ops:
  7.2 4.9 copy-start.3
  7.2 108.2 %all-reduce.131.cloned.1.call-start = ((), (), s32[]{:S(2)}) async-start(), calls=%async_computation | async-start | bytes 524288 | tf_op jit(solution)/shard_map/psum | solution.py:112
  7.9 4.2 copy-start.1
  9.4 10.2 %collective-permute-start.1 = (bf16[64,1,16,128]{3,0,2,1:T(8,128)(2,1)S(1)}, bf16[64,1,16,128]{3,0,2,1:T(8,128)(2,1)S(1)}, u32[]{:S(2)}, u32[]{:S(2)}) collective-permute-start(bf16[64,1,16,128]{3,0,2,1:T(8,128)(2,1)S(1)} %slice.17541), channel_id=1, source_target_pairs={{1,0},{2,1},{3,2},{4,3},{5,4},{6,5},{7,6},{8,7},{9,8},{10,9},{11,1... | collective-permute-start | bytes 786440 | tf_op jit(solution)/shard_map/ppermute | solution.py:15
  9.5 3.5 copy-start.2
  9.5 10.2 %collective-permute-start = (bf16[64,1,16,128]{3,0,2,1:T(8,128)(2,1)S(1)}, bf16[64,1,16,128]{3,0,2,1:T(8,128)(2,1)S(1)}, u32[]{:S(2)}, u32[]{:S(2)}) collective-permute-start(bf16[64,1,16,128]{3,0,2,1:T(8,128)(2,1)S(1)} %bitcast.7046), channel_id=1, source_target_pairs={{0,1},{1,2},{2,3},{3,4},{4,5},{5,6},{6,7},{7,8},{8,9},{9,10},{10,1... | collective-permute-start | bytes 786440 | tf_op jit(solution)/shard_map/ppermute | solution.py:14
  12.9 6.8 copy-start
  23.9 110.4 %copy-start.11 = (f32[8]{0:T(128)S(1)}, f32[8]{0:T(128)}, u32[]{:S(2)}) copy-start(f32[8]{0:T(128)} %constant.13709.clone.1) | copy-start | bytes 100
  23.9 111.1 %copy-start.10 = (f32[8]{0:T(128)S(1)}, f32[8]{0:T(128)}, u32[]{:S(2)}) copy-start(f32[8]{0:T(128)} %constant.13724.clone.1) | copy-start | bytes 100
  23.9 111.9 %copy-start.9 = (f32[8]{0:T(128)S(1)}, f32[8]{0:T(128)}, u32[]{:S(2)}) copy-start(f32[8]{0:T(128)} %constant.13725.clone.1) | copy-start | bytes 100
  23.9 112.7 %copy-start.8 = (f32[8]{0:T(128)S(1)}, f32[8]{0:T(128)}, u32[]{:S(2)}) copy-start(f32[8]{0:T(128)} %constant.13726.clone.1) | copy-start | bytes 100
  24.0 113.5 %copy-start.7 = (f32[8]{0:T(128)S(1)}, f32[8]{0:T(128)}, u32[]{:S(2)}) copy-start(f32[8]{0:T(128)} %constant.13727.clone.1) | copy-start | bytes 100
  24.0 114.2 %copy-start.6 = (f32[8]{0:T(128)S(1)}, f32[8]{0:T(128)}, u32[]{:S(2)}) copy-start(f32[8]{0:T(128)} %constant.13728.clone.1) | copy-start | bytes 100
  24.0 115.0 %copy-start.5 = (f32[8]{0:T(128)S(1)}, f32[8]{0:T(128)}, u32[]{:S(2)}) copy-start(f32[8]{0:T(128)} %constant.13729.clone.1) | copy-start | bytes 100
  24.0 115.8 %copy-start.4 = (f32[8]{0:T(128)S(1)}, f32[8]{0:T(128)}, u32[]{:S(2)}) copy-start(f32[8]{0:T(128)} %constant.13730.clone.1) | copy-start | bytes 100
Sparse Core Ops, SparseCore 0:
  22.6 92.7 all-reduce.130
where the time goes:
time: 937 us; the launch traced here: 922 us
  matrix products  245 us (26%)
  local copies, waits for them, and re-layouts  242 us (26%)
  between operations  178 us (19%)
  other arithmetic  166 us (18%)
  waiting for transfers between devices  88.5 us (9%)
    dot_general x605, matrix products, exact_dot(): return jnp.dot(left_mat, right_mat, precision=lax.Precision.HIGHEST)  242 us
    another operation x423, other arithmetic  157 us
    slice x224, local copies, waits for them, and re-layouts, leaf_factor(): pivot = jnp.sqrt(residue[column])  134 us
    psum x1, waiting for transfers between devices, shards(): gram = lax.psum(local_gram, 'blk') / cell_total  88.5 us
    slice x64, local copies, waits for them, and re-layouts, leaf_factor(): solved = (target - exact_dot(lower[row, :], inverse)) / lower[row, row]  42.5 us
    scatter x256, local copies, waits for them, and re-layouts, leaf_factor(): lower.at[:, column].set(jnp.where(row_ids >= column, residue / pivot, 0.0))  21 us
    another operation x256, local copies, waits for them, and re-layouts  20.9 us
  transfers between devices with their start and end apart: 3, of which 1 were waited for; matrix products, arithmetic and copies ran while one was open for 1% of the time, Pallas kernels for 0%

commit v1 on v0

--- a/solution.py
+++ b/solution.py
@@ -109,7 +109,7 @@
     )
     cell_total = lax.axis_size("blk") * stacked.shape[1]
     local_gram = gram_term(stacked, stacked)
-    gram = lax.psum(local_gram, "blk") / cell_total
+    gram = jnp.sum(jax.lax.all_gather(local_gram, "blk"), axis=0) / cell_total
     lower, inverse_lower = lower_factor(gram)
     factor = lower.T
     inverse_high = inverse_lower.astype(jnp.bfloat16)

time: 937 us -> 896 us (0.956)
  waiting for transfers between devices: 88.5 us -> 47.3 us
  local copies, waits for them, and re-layouts: 242 us -> 230 us
    psum x1 -> x0, waiting for transfers between devices: 88.5 us -> none  [shards(): gram = lax.psum(local_gram, 'blk') / cell_total]
    all_gather x0 -> x1, waiting for transfers between devices: none -> 44 us  [shards(): gram = jnp.sum(jax.lax.all_gather(local_gram, 'blk'), axis=0) / cell_total]
    slice x32 -> x0, local copies, waits for them, and re-layouts: 10.9 us -> none  [leaf_factor(): residue = matrix[:, column] - exact_dot(lower, lower[column, :])]
  transfers between devices with their start and end apart: 3 -> 3, of which waited for: 1 -> 3; matrix products, arithmetic and copies ran while one was open for 1% -> 1% of each run, Pallas kernels for 0% -> 0%
where the time goes in v1:
time: 896 us; the launch traced here: 881 us
  matrix products  254 us (28%)
  local copies, waits for them, and re-layouts  230 us (26%)
  between operations  179 us (20%)
  other arithmetic  168 us (19%)
  waiting for transfers between devices  47.3 us (5%)
    dot_general x605, matrix products, exact_dot(): return jnp.dot(left_mat, right_mat, precision=lax.Precision.HIGHEST)  251 us
    another operation x423, other arithmetic  157 us
    slice x224, local copies, waits for them, and re-layouts, leaf_factor(): pivot = jnp.sqrt(residue[column])  134 us
    all_gather x1, waiting for transfers between devices, shards(): gram = jnp.sum(jax.lax.all_gather(local_gram, 'blk'), axis=0) / cell_total  44 us
    slice x64, local copies, waits for them, and re-layouts, leaf_factor(): solved = (target - exact_dot(lower[row, :], inverse)) / lower[row, row]  42.3 us
    another operation x256, local copies, waits for them, and re-layouts  20.9 us
    scatter x256, local copies, waits for them, and re-layouts, leaf_factor(): lower.at[:, column].set(jnp.where(row_ids >= column, residue / pivot, 0.0))  20.2 us
  transfers between devices with their start and end apart: 3, of which 3 were waited for; matrix products, arithmetic and copies ran while one was open for 1% of the time, Pallas kernels for 0%

profile of v1, /device:TPU:1, one launch (start us, length us, event | category | flops | bytes accessed | tf_op | source)
XLA Modules:
  0.0 880.6 jit_solution(14115165442604494694)
XLA Ops:
  7.9 1.4 multiply_reduce_fusion
  9.5 2.6 collective-permute-start
  14.9 1.2 collective-permute-done.1
  16.1 2.1 collective-permute-done
  19.6 1.4 convolution_bitcast_fusion
  25.8 1.5 pad_maximum_fusion
  27.3 2.9 copy.790
  30.2 44.0 %all-gather.3.cloned.1.call-done = f32[4096,256]{1,0:T(8,128)} async-done(((f32[256,256]{1,0:T(8,128)}), f32[4096,256]{1,0:T(8,128)}) %all-gather.3.cloned.1.call-update) | async-done | bytes 4194320 | tf_op jit(solution)/shard_map/all_gather | solution.py:112
  74.2 2.5 reduce_sum.19
  121.4 0.8 fusion.51
  144.3 0.8 fusion.76
  146.7 0.8 fusion.85
  171.5 0.8 fusion.116
  196.3 0.8 fusion.147
  220.0 0.8 fusion.175
  242.9 0.8 fusion.200
  245.3 0.8 fusion.209
  270.1 0.8 fusion.240
  295.3 0.8 fusion.271
  319.1 0.8 fusion.299
  344.4 0.8 fusion.333
  369.0 0.8 fusion.364
  393.8 0.8 fusion.395
  440.8 0.8 fusion.448
  443.2 0.8 fusion.457
  468.1 0.8 fusion.488
  493.5 0.8 fusion.519
  517.2 0.8 fusion.547
  542.5 0.8 fusion.581
  567.3 0.8 fusion.612
  589.7 0.8 fusion.634
  592.1 0.8 fusion.643
  615.8 0.8 fusion.671
  641.1 0.8 fusion.705
  663.5 0.8 fusion.727
  665.9 0.8 fusion.736
  688.7 0.8 fusion.758
  691.1 0.8 fusion.767
  714.9 0.8 fusion.795
  737.7 0.8 fusion.820
  740.2 0.8 fusion.829
  764.8 0.8 fusion.860
  789.7 0.8 fusion.891
  813.7 0.8 fusion.919
  839.1 0.8 fusion.953
  864.5 0.8 fusion.984
  868.2 0.8 copy.792
  871.6 1.8 copy.795
  (2198 shorter events, 608.8 us)
Async XLA Ops:
  7.2 4.9 copy-start.3
  7.2 67.0 %all-gather.3.cloned.1.call-start = ((), (), s32[]{:S(2)}) async-start(), calls=%async_computation | async-start | bytes 4456448 | tf_op jit(solution)/shard_map/all_gather | solution.py:112
  7.9 4.2 copy-start.1
  9.4 6.7 collective-permute-start.1
  9.5 3.5 copy-start.2
  9.5 8.7 collective-permute-start
  12.9 5.4 copy-start
  74.2 20.4 %copy-start.11 = (f32[8]{0:T(128)S(1)}, f32[8]{0:T(128)}, u32[]{:S(2)}) copy-start(f32[8]{0:T(128)} %constant.13709.clone.1) | copy-start | bytes 100
  74.2 21.1 %copy-start.10 = (f32[8]{0:T(128)S(1)}, f32[8]{0:T(128)}, u32[]{:S(2)}) copy-start(f32[8]{0:T(128)} %constant.13724.clone.1) | copy-start | bytes 100
  74.2 21.9 %copy-start.9 = (f32[8]{0:T(128)S(1)}, f32[8]{0:T(128)}, u32[]{:S(2)}) copy-start(f32[8]{0:T(128)} %constant.13725.clone.1) | copy-start | bytes 100
  74.2 22.7 %copy-start.8 = (f32[8]{0:T(128)S(1)}, f32[8]{0:T(128)}, u32[]{:S(2)}) copy-start(f32[8]{0:T(128)} %constant.13726.clone.1) | copy-start | bytes 100
  74.2 23.5 %copy-start.7 = (f32[8]{0:T(128)S(1)}, f32[8]{0:T(128)}, u32[]{:S(2)}) copy-start(f32[8]{0:T(128)} %constant.13727.clone.1) | copy-start | bytes 100
  74.2 24.3 %copy-start.6 = (f32[8]{0:T(128)S(1)}, f32[8]{0:T(128)}, u32[]{:S(2)}) copy-start(f32[8]{0:T(128)} %constant.13728.clone.1) | copy-start | bytes 100
  74.2 25.1 %copy-start.5 = (f32[8]{0:T(128)S(1)}, f32[8]{0:T(128)}, u32[]{:S(2)}) copy-start(f32[8]{0:T(128)} %constant.13729.clone.1) | copy-start | bytes 100
  74.2 25.9 %copy-start.4 = (f32[8]{0:T(128)S(1)}, f32[8]{0:T(128)}, u32[]{:S(2)}) copy-start(f32[8]{0:T(128)} %constant.13730.clone.1) | copy-start | bytes 100
Sparse Core Ops, SparseCore 0:
  21.2 52.9 all-gather.2
